TPU v7x, 32 devices: a whole 2x2x4 slice. The times are simulated.
32 devices in a mesh: segment: 2 (over x), dp: 16 (over z, y, core).
Axes of the slice: x: 2, y: 2, z: 4, core: 2. Of those that a mesh axis runs over, the one named last changes fastest.
Arguments:
- latents: bfloat16 [2, 2048, 3072], P(None, 'dp'), may hold values from -70 to 70
- proj: bfloat16 [2, 3072, 1536], P('segment', 'dp'), may hold values from -0.109375 to 0.109375
- temper: float32 [2, 12], P('segment'), may hold values from 0.3 to 24
- blocks: int32 [2, 32, 12, 2], P(None, 'dp'), may hold values from 0 to 5
Outputs:
- states: bfloat16 [2, 2, 2048, 3072], P('segment', None, 'dp')
All inputs are finite; a program needn't handle non-finite values.
Results may differ from a plain program's by a relative error of at most 0.013.
Values may be sent and summed in bfloat16 or wider, within the bound.
A program may use at most 64 MiB of HBM per device.

v0:
```python
import math

import jax
import jax.numpy as jnp
from jax import lax
from jax.sharding import PartitionSpec as P

BLOCK = 64
SEL = 2


epsilon = 1e-06


def from_behind(value, axis, by):
    count = lax.axis_size(axis)
    pairs = [(i, i + by) for i in range(count) if 0 <= i + by < count]
    return lax.ppermute(value, axis, pairs)


def unit_heads(values, head_count):
    shaped = values.astype(jnp.float32).reshape(values.shape[:-1] + (head_count, -1))
    return (shaped * lax.rsqrt(jnp.mean(shaped * shaped, axis=-1, keepdims=True) + epsilon)).astype(
        jnp.bfloat16
    )


def on_device(latents, proj, temper, blocks):
    segment_count = lax.axis_size("segment")
    segment_idx = lax.axis_index("segment")
    dp_count = lax.axis_size("dp")
    dp_index = lax.axis_index("dp")
    micro_count, tok_rows, width = latents.shape
    head_count = temper.shape[1]
    feat_width = proj.shape[2]
    head_size = feat_width // head_count
    per_dev = tok_rows // BLOCK
    total_blocks = tok_rows * dp_count // BLOCK
    seq_blocks = min(4096, tok_rows * dp_count) // BLOCK
    weight = lax.all_gather(proj[0], "dp", axis=0, tiled=True)
    score_scale = temper[0] * (1.0 / math.sqrt(head_size))
    diag = jnp.eye(BLOCK, dtype=bool)

    def project(hidden):
        h_float = hidden.astype(jnp.float32)
        normed = (
            h_float * lax.rsqrt(jnp.mean(h_float * h_float, axis=-1, keepdims=True) + epsilon)
        ).astype(jnp.bfloat16)
        return jnp.dot(normed, weight, preferred_element_type=jnp.float32).astype(jnp.bfloat16)

    def attend(values, before, after, chosen):
        window = jnp.concatenate([before, values, after], axis=0).reshape(
            3 * per_dev, BLOCK, feat_width
        )
        keys_win = unit_heads(window, head_count)
        vals_win = window.reshape(3 * per_dev, BLOCK, head_count, head_size)
        own_keys = keys_win[per_dev : 2 * per_dev]
        own_vals = vals_win[per_dev : 2 * per_dev]
        onehot = (chosen[..., None] == jnp.arange(3 * per_dev, dtype=jnp.int32)).astype(
            jnp.bfloat16
        )
        key_pick = jnp.einsum(
            "qhsw,wjhd->qhsjd", onehot, keys_win, preferred_element_type=jnp.float32
        ).astype(jnp.bfloat16)
        val_pick = jnp.einsum(
            "qhsw,wjhd->qhsjd", onehot, vals_win, preferred_element_type=jnp.float32
        ).astype(jnp.bfloat16)
        query_block = dp_index * per_dev + jnp.arange(per_dev, dtype=jnp.int32)
        absolute = (dp_index - 1) * per_dev + chosen
        usable = (
            (absolute >= 0)
            & (absolute < total_blocks)
            & (absolute // seq_blocks == (query_block // seq_blocks)[:, None, None])
        )
        same_block = absolute == query_block[:, None, None]
        own_stack = jnp.transpose(own_keys, (0, 2, 1, 3))[:, :, None]
        all_keys = jnp.concatenate([own_stack, key_pick], axis=2)
        own_vstack = jnp.transpose(own_vals, (0, 2, 1, 3))[:, :, None]
        all_vals = jnp.concatenate([own_vstack, val_pick], axis=2)
        scores = jnp.einsum(
            "qihd,qhsjd->qhisj", own_keys, all_keys, preferred_element_type=jnp.float32
        )
        scores = scores * score_scale[None, :, None, None, None]
        ones_col = jnp.ones(usable.shape[:2] + (1,), dtype=bool)
        usable_all = jnp.concatenate([ones_col, usable], axis=2)
        same_all = jnp.concatenate([ones_col, same_block], axis=2)
        keep = usable_all[:, :, None, :, None] & ~(
            same_all[:, :, None, :, None] & diag[None, None, :, None, :]
        )
        scores = jnp.where(keep, scores, -jnp.inf)
        flat = scores.reshape(per_dev, head_count, BLOCK, (1 + SEL) * BLOCK)
        weights = jax.nn.softmax(flat, axis=-1).astype(jnp.bfloat16)
        weights = weights.reshape(per_dev, head_count, BLOCK, 1 + SEL, BLOCK)
        mixed = jnp.einsum(
            "qhisj,qhsjd->qihd", weights, all_vals, preferred_element_type=jnp.float32
        )
        return mixed.reshape(tok_rows, feat_width).astype(jnp.bfloat16)

    def finish(hidden, mixed):
        back = lax.dot_general(
            mixed, weight, (((1,), (1,)), ((), ())), preferred_element_type=jnp.float32
        )
        return (hidden.astype(jnp.float32) + back).astype(jnp.bfloat16)

    turns = micro_count + segment_count - 1

    def one_turn(turn, carry):
        incoming, states = carry
        slot_now = turn - segment_idx
        active = (slot_now >= 0) & (slot_now < micro_count)
        slot_safe = jnp.clip(slot_now, 0, micro_count - 1)
        first_input = lax.dynamic_index_in_dim(latents, slot_safe, 0, keepdims=False)
        hidden = jnp.where(segment_idx == 0, first_input, incoming)
        values = lax.cond(
            active, lambda: project(hidden), lambda: jnp.zeros((tok_rows, feat_width), jnp.bfloat16)
        )
        beside = []
        for offset in (1, -1):
            beside.append(from_behind(values, "dp", offset))
        chosen = lax.dynamic_index_in_dim(blocks, slot_safe, 0, keepdims=False)
        result = lax.cond(
            active,
            lambda: finish(hidden, attend(values, beside[0], beside[1], chosen)),
            lambda: jnp.zeros((tok_rows, width), jnp.bfloat16),
        )
        previous = lax.dynamic_index_in_dim(states, slot_safe, 0, keepdims=False)
        states = lax.dynamic_update_index_in_dim(
            states, jnp.where(active, result, previous), slot_safe, 0
        )
        incoming = from_behind(result, "segment", 1)
        return (incoming, states)

    start_states = jnp.zeros((micro_count, tok_rows, width), jnp.bfloat16)
    start_input = jnp.zeros((tok_rows, width), jnp.bfloat16)
    final_input, states = lax.fori_loop(0, turns, one_turn, (start_input, start_states))
    return states[None]


def solution(mesh):
    placed = (
        P(None, "dp", None),
        P("segment", "dp", None),
        P("segment", None),
        P(None, "dp", None, None),
    )
    return jax.shard_map(
        on_device,
        mesh=mesh,
        in_specs=placed,
        out_specs=P("segment", None, "dp", None),
        check_vma=False,
    )
```

profile of v0, /device:TPU:14, one launch (start us, length us, event | category | flops | bytes accessed | tf_op | source)
XLA Modules:
  0.0 287.3 jit_solution(14086132831907205156)
XLA Ops:
  8.5 81.9 %all-gather.3.cloned.1.call-done = bf16[1,3072,1536]{2,1,0:T(8,128)(2,1)} async-done(((bf16[1,192,1536]{2,1,0:T(8,128)(2,1)}), bf16[1,3072,1536]{2,1,0:T(8,128)(2,1)}) %all-gather.3.cloned.1.call-update) | async-done | bytes 9437200 | tf_op jit(solution)/shard_map/all_gather | solution.py:40
  90.5 1.3 broadcast_in_dim.40
  91.8 188.6 %while.17 = (s32[]{:T(128)}, bf16[128,3072]{1,0:T(8,128)(2,1)S(1)}, bf16[2,128,3072]{2,1,0:T(8,128)(2,1)}, s32[]{:T(128)}, pred[]{:T(512)}, /*index=5*/bf16[2,12...) while((s32[]{:T(128)}, bf16[128,3072]{1,0:T(8,128)(2,1)S(1)}, ...), condition=%wide.region_9.10_spmd.clone, body=%wide.region_0.9_spmd.clone.sunk | while | flops 2592578560 | bytes 95464112 | solution.py:135
  93.1 3.2 %collective-permute-start.1 = (bf16[128,1536]{1,0:T(8,128)(2,1)S(1)}, bf16[128,1536]{1,0:T(8,128)(2,1)S(1)}, u32[]{:S(2)}, u32[]{:S(2)}) collective-permute-start(bf16[128,1536]{1,0:T(8,128)(2,1)S(1)} %get-tuple-element.445), channel_id=1, source_target_pairs={{1,0},{2,1},{3,2},{4,3},{5,4},{6,5},{7,6},{8,7},{9,8},{10,9},{11,1... | collective-permute-start | bytes 1179656 | tf_op jit(solution)/shard_map/while/body/eval_jaxpr/ppermute | solution.py:18
  96.3 1.9 collective-permute-start
  98.3 7.6 %collective-permute-done.1 = bf16[128,1536]{1,0:T(8,128)(2,1)S(1)} collective-permute-done((bf16[128,1536]{1,0:T(8,128)(2,1)S(1)}, bf16[128,1536]{1,0:T(8,128)(2,1)S(1)}, u32[]{:S(2)}, u32[]{:S(2)}) %collective-permute-start.1) | collective-permute-done | bytes 393248 | tf_op jit(solution)/shard_map/while/body/eval_jaxpr/ppermute | solution.py:18
  105.9 2.0 collective-permute-done
  108.8 1.3 collective-permute-start.2
  112.4 40.3 %collective-permute-done.2 = bf16[128,3072]{1,0:T(8,128)(2,1)S(1)} collective-permute-done((bf16[128,3072]{1,0:T(8,128)(2,1)}, bf16[128,3072]{1,0:T(8,128)(2,1)S(1)}, u32[]{:S(2)}, u32[]{:S(2)}) %collective-permute-start.2) | collective-permute-done | bytes 786464 | tf_op jit(solution)/shard_map/while/body/eval_jaxpr/ppermute | solution.py:18
  153.9 5.4 %conditional.6 = (bf16[128,1536]{1,0:T(8,128)(2,1)S(1)}) conditional(s32[]{:T(128)} %convert_element_type.101, () %tuple.61, (bf16[128,3072]{1,0:T(8,128)(2,1)S(1)}, bf16[3072,1536]{1,0:T(8,128)(2,1)}) %tuple.62), branch_computations={%region_1.1_spmd, %region_2.3_spmd} | conditional | flops 1210515584 | bytes 11405320 | solution.py:114
  154.2 5.1 %convolution_convert_fusion = bf16[128,1536]{1,0:T(8,128)(2,1)S(1)} fusion(bf16[3072,1536]{1,0:T(8,128)(2,1)} %get-tuple-element.270, bf16[128,3072]{1,0:T(8,128)(2,1)S(1)} %get-tuple-element.269, f32[128]{0:T(128)S(1)} %add_rsqrt_fusion), kind=kOutput, calls=%fused_computation.1 | convolution fusion | flops 1209335808 | bytes 10617344 | tf_op jit(solution)/shard_map/while/body/eval_jaxpr/cond/branch_1_fun/dot_general | solution.py:49
  159.3 4.8 %collective-permute-start.1 = (bf16[128,1536]{1,0:T(8,128)(2,1)S(1)}, bf16[128,1536]{1,0:T(8,128)(2,1)S(1)}, u32[]{:S(2)}, u32[]{:S(2)}) collective-permute-start(bf16[128,1536]{1,0:T(8,128)(2,1)S(1)} %get-tuple-element.445), channel_id=1, source_target_pairs={{1,0},{2,1},{3,2},{4,3},{5,4},{6,5},{7,6},{8,7},{9,8},{10,9},{11,1... | collective-permute-start | bytes 1179656 | tf_op jit(solution)/shard_map/while/body/eval_jaxpr/ppermute | solution.py:18
  164.1 1.9 collective-permute-start
  166.0 7.6 %collective-permute-done.1 = bf16[128,1536]{1,0:T(8,128)(2,1)S(1)} collective-permute-done((bf16[128,1536]{1,0:T(8,128)(2,1)S(1)}, bf16[128,1536]{1,0:T(8,128)(2,1)S(1)}, u32[]{:S(2)}, u32[]{:S(2)}) %collective-permute-start.1) | collective-permute-done | bytes 393248 | tf_op jit(solution)/shard_map/while/body/eval_jaxpr/ppermute | solution.py:18
  173.6 1.5 collective-permute-done
  175.1 23.0 %conditional.7 = (bf16[128,3072]{1,0:T(8,128)(2,1)}) conditional(s32[]{:T(128)} %convert_element_type.101, () %tuple.60, (bf16[128,3072]{1,0:T(8,128)(2,1)S(1)}, bf16[128,1536]{1,0:T(8,128)(2,1)S(1)}, bf16[128,1536]{1,0:T(8,128)(2,1)}, bf16[128,1536]{1,0:T(8,128)(2,1)S(1)}, s32[2,2,12,2]{2,3,1,0:T(2,128)}, /*index=5*/s32[]{:T(128)}, s32[]{:T(128)}, ...), branch_computations={%region_4.4_spmd, %region_5.8_spmd} | conditional | flops 1381276544 | bytes 71442176 | solution.py:121
  182.2 1.7 reshape.61
  184.0 3.1 %fusion.12 = bf16[12,64,128,2,2]{2,4,3,1,0:T(2,128)(2,1)S(1)} fusion(bf16[6,64,12,128,1]{3,2,1,0,4:T(8,128)(2,1)} %reshape.61, pred[2,12,2,6,1]{3,2,1,0,4:T(4,128)(4,1)S(1)} %compare_bitcast_fusion), kind=kOutput, calls=%fused_computation.22 | convolution fusion | flops 4718592 | bytes 1966368 | tf_op jit(solution)/shard_map/while/body/eval_jaxpr/cond/branch_1_fun/qhsw,wjhd->qhsjd/dot_general | solution.py:65
  194.1 4.1 %fusion.6 = bf16[128,3072]{1,0:T(8,128)(2,1)} fusion(bf16[3072,1536]{1,0:T(8,128)(2,1)S(1)} %bitcast.65, bf16[128,3072]{1,0:T(8,128)(2,1)S(1)} %get-tuple-element.271, bf16[16,8,12,128]{3,2,1,0:T(8,128)(2,1)S(1)} %bitcast.66), kind=kOutput, calls=%fused_computation.9 | convolution fusion | flops 1209139200 | bytes 11403264 | tf_op jit(solution)/shard_map/while/body/eval_jaxpr/cond/branch_1_fun/dot_general | solution.py:100
  200.7 2.2 bitcast_dynamic-update-slice_fusion.2
  202.9 13.6 %collective-permute-done.2 = bf16[128,3072]{1,0:T(8,128)(2,1)S(1)} collective-permute-done((bf16[128,3072]{1,0:T(8,128)(2,1)}, bf16[128,3072]{1,0:T(8,128)(2,1)S(1)}, u32[]{:S(2)}, u32[]{:S(2)}) %collective-permute-start.2) | collective-permute-done | bytes 786464 | tf_op jit(solution)/shard_map/while/body/eval_jaxpr/ppermute | solution.py:18
  217.7 5.4 %conditional.6 = (bf16[128,1536]{1,0:T(8,128)(2,1)S(1)}) conditional(s32[]{:T(128)} %convert_element_type.101, () %tuple.61, (bf16[128,3072]{1,0:T(8,128)(2,1)S(1)}, bf16[3072,1536]{1,0:T(8,128)(2,1)}) %tuple.62), branch_computations={%region_1.1_spmd, %region_2.3_spmd} | conditional | flops 1210515584 | bytes 11405320 | solution.py:114
  217.9 5.1 %convolution_convert_fusion = bf16[128,1536]{1,0:T(8,128)(2,1)S(1)} fusion(bf16[3072,1536]{1,0:T(8,128)(2,1)} %get-tuple-element.270, bf16[128,3072]{1,0:T(8,128)(2,1)S(1)} %get-tuple-element.269, f32[128]{0:T(128)S(1)} %add_rsqrt_fusion), kind=kOutput, calls=%fused_computation.1 | convolution fusion | flops 1209335808 | bytes 10617344 | tf_op jit(solution)/shard_map/while/body/eval_jaxpr/cond/branch_1_fun/dot_general | solution.py:49
  223.1 5.5 %collective-permute-start.1 = (bf16[128,1536]{1,0:T(8,128)(2,1)S(1)}, bf16[128,1536]{1,0:T(8,128)(2,1)S(1)}, u32[]{:S(2)}, u32[]{:S(2)}) collective-permute-start(bf16[128,1536]{1,0:T(8,128)(2,1)S(1)} %get-tuple-element.445), channel_id=1, source_target_pairs={{1,0},{2,1},{3,2},{4,3},{5,4},{6,5},{7,6},{8,7},{9,8},{10,9},{11,1... | collective-permute-start | bytes 1179656 | tf_op jit(solution)/shard_map/while/body/eval_jaxpr/ppermute | solution.py:18
  228.6 1.9 collective-permute-start
  230.5 7.6 %collective-permute-done.1 = bf16[128,1536]{1,0:T(8,128)(2,1)S(1)} collective-permute-done((bf16[128,1536]{1,0:T(8,128)(2,1)S(1)}, bf16[128,1536]{1,0:T(8,128)(2,1)S(1)}, u32[]{:S(2)}, u32[]{:S(2)}) %collective-permute-start.1) | collective-permute-done | bytes 393248 | tf_op jit(solution)/shard_map/while/body/eval_jaxpr/ppermute | solution.py:18
  239.1 23.0 %conditional.7 = (bf16[128,3072]{1,0:T(8,128)(2,1)}) conditional(s32[]{:T(128)} %convert_element_type.101, () %tuple.60, (bf16[128,3072]{1,0:T(8,128)(2,1)S(1)}, bf16[128,1536]{1,0:T(8,128)(2,1)S(1)}, bf16[128,1536]{1,0:T(8,128)(2,1)}, bf16[128,1536]{1,0:T(8,128)(2,1)S(1)}, s32[2,2,12,2]{2,3,1,0:T(2,128)}, /*index=5*/s32[]{:T(128)}, s32[]{:T(128)}, ...), branch_computations={%region_4.4_spmd, %region_5.8_spmd} | conditional | flops 1381276544 | bytes 71442176 | solution.py:121
  246.2 1.7 reshape.61
  248.0 3.1 %fusion.12 = bf16[12,64,128,2,2]{2,4,3,1,0:T(2,128)(2,1)S(1)} fusion(bf16[6,64,12,128,1]{3,2,1,0,4:T(8,128)(2,1)} %reshape.61, pred[2,12,2,6,1]{3,2,1,0,4:T(4,128)(4,1)S(1)} %compare_bitcast_fusion), kind=kOutput, calls=%fused_computation.22 | convolution fusion | flops 4718592 | bytes 1966368 | tf_op jit(solution)/shard_map/while/body/eval_jaxpr/cond/branch_1_fun/qhsw,wjhd->qhsjd/dot_general | solution.py:65
  258.1 4.1 %fusion.6 = bf16[128,3072]{1,0:T(8,128)(2,1)} fusion(bf16[3072,1536]{1,0:T(8,128)(2,1)S(1)} %bitcast.65, bf16[128,3072]{1,0:T(8,128)(2,1)S(1)} %get-tuple-element.271, bf16[16,8,12,128]{3,2,1,0:T(8,128)(2,1)S(1)} %bitcast.66), kind=kOutput, calls=%fused_computation.9 | convolution fusion | flops 1209139200 | bytes 11403264 | tf_op jit(solution)/shard_map/while/body/eval_jaxpr/cond/branch_1_fun/dot_general | solution.py:100
  264.6 2.2 bitcast_dynamic-update-slice_fusion.2
  266.8 13.6 %collective-permute-done.2 = bf16[128,3072]{1,0:T(8,128)(2,1)S(1)} collective-permute-done((bf16[128,3072]{1,0:T(8,128)(2,1)}, bf16[128,3072]{1,0:T(8,128)(2,1)S(1)}, u32[]{:S(2)}, u32[]{:S(2)}) %collective-permute-start.2) | collective-permute-done | bytes 786464 | tf_op jit(solution)/shard_map/while/body/eval_jaxpr/ppermute | solution.py:18
  (118 shorter events, 44.2 us)
Async XLA Ops:
  6.5 83.9 %all-gather.3.cloned.1.call-start = ((), (), s32[]{:S(2)}) async-start(), calls=%async_computation | async-start | bytes 10027008 | tf_op jit(solution)/shard_map/all_gather | solution.py:40
  93.1 12.8 %collective-permute-start.1 = (bf16[128,1536]{1,0:T(8,128)(2,1)S(1)}, bf16[128,1536]{1,0:T(8,128)(2,1)S(1)}, u32[]{:S(2)}, u32[]{:S(2)}) collective-permute-start(bf16[128,1536]{1,0:T(8,128)(2,1)S(1)} %get-tuple-element.445), channel_id=1, source_target_pairs={{1,0},{2,1},{3,2},{4,3},{5,4},{6,5},{7,6},{8,7},{9,8},{10,9},{11,1... | collective-permute-start | bytes 1179656 | tf_op jit(solution)/shard_map/while/body/eval_jaxpr/ppermute | solution.py:18
  96.3 11.5 %collective-permute-start = (bf16[128,1536]{1,0:T(8,128)(2,1)S(1)}, bf16[128,1536]{1,0:T(8,128)(2,1)}, u32[]{:S(2)}, u32[]{:S(2)}) collective-permute-start(bf16[128,1536]{1,0:T(8,128)(2,1)S(1)} %get-tuple-element.445), channel_id=1, source_target_pairs={{0,1},{1,2},{2,3},{3,4},{4,5},{5,6},{6,7},{7,8},{8,9},{9,10},{10,1... | collective-permute-start | bytes 1179656 | tf_op jit(solution)/shard_map/while/body/eval_jaxpr/ppermute | solution.py:18
  108.8 43.9 %collective-permute-start.2 = (bf16[128,3072]{1,0:T(8,128)(2,1)}, bf16[128,3072]{1,0:T(8,128)(2,1)S(1)}, u32[]{:S(2)}, u32[]{:S(2)}) collective-permute-start(bf16[128,3072]{1,0:T(8,128)(2,1)} %get-tuple-element.446), channel_id=1, source_target_pairs={{0,16},{1,17},{2,18},{3,19},{4,20},{5,21},{6,22},{7,23},{8,24},{9,... | collective-permute-start | bytes 2359304 | tf_op jit(solution)/shard_map/while/body/eval_jaxpr/ppermute | solution.py:18
  159.3 14.3 %collective-permute-start.1 = (bf16[128,1536]{1,0:T(8,128)(2,1)S(1)}, bf16[128,1536]{1,0:T(8,128)(2,1)S(1)}, u32[]{:S(2)}, u32[]{:S(2)}) collective-permute-start(bf16[128,1536]{1,0:T(8,128)(2,1)S(1)} %get-tuple-element.445), channel_id=1, source_target_pairs={{1,0},{2,1},{3,2},{4,3},{5,4},{6,5},{7,6},{8,7},{9,8},{10,9},{11,1... | collective-permute-start | bytes 1179656 | tf_op jit(solution)/shard_map/while/body/eval_jaxpr/ppermute | solution.py:18
  164.1 11.0 %collective-permute-start = (bf16[128,1536]{1,0:T(8,128)(2,1)S(1)}, bf16[128,1536]{1,0:T(8,128)(2,1)}, u32[]{:S(2)}, u32[]{:S(2)}) collective-permute-start(bf16[128,1536]{1,0:T(8,128)(2,1)S(1)} %get-tuple-element.445), channel_id=1, source_target_pairs={{0,1},{1,2},{2,3},{3,4},{4,5},{5,6},{6,7},{7,8},{8,9},{9,10},{10,1... | collective-permute-start | bytes 1179656 | tf_op jit(solution)/shard_map/while/body/eval_jaxpr/ppermute | solution.py:18
  184.0 3.3 %copy-start = (f32[6,64,12]{1,2,0:T(8,128)S(1)}, f32[6,64,12]{1,2,0:T(8,128)}, u32[]{:S(2)}) copy-start(f32[6,64,12]{1,2,0:T(8,128)} %add_rsqrt_fusion.1) | copy-start | bytes 55300 | tf_op jit(solution)/shard_map/while/body/eval_jaxpr/cond
  188.9 1.4 copy-start.2
  188.9 1.4 copy-start.3
  188.9 1.4 copy-start.4
  190.0 3.6 %slice-start = ((s8[9437184]{0:T(1024)(128)(4,1)}), s8[4194304]{0:T(1024)(128)(4,1)S(1)}, s32[]{:S(2)}) async-start(s8[9437184]{0:T(1024)(128)(4,1)} %bitcast.64), calls=%async_computation.1 | async-start | bytes 8388608 | tf_op jit(solution)/shard_map/while/body/eval_jaxpr/cond
  190.3 3.4 %slice-start.1 = ((s8[9437184]{0:T(1024)(128)(4,1)}), s8[4194304]{0:T(1024)(128)(4,1)S(1)}, s32[]{:S(2)}) async-start(s8[9437184]{0:T(1024)(128)(4,1)} %bitcast.64), calls=%async_computation.2 | async-start | bytes 8388608 | tf_op jit(solution)/shard_map/while/body/eval_jaxpr/cond
  191.1 1.5 copy-start.1
  192.6 1.5 slice-start.2
  198.2 18.3 %collective-permute-start.2 = (bf16[128,3072]{1,0:T(8,128)(2,1)}, bf16[128,3072]{1,0:T(8,128)(2,1)S(1)}, u32[]{:S(2)}, u32[]{:S(2)}) collective-permute-start(bf16[128,3072]{1,0:T(8,128)(2,1)} %get-tuple-element.446), channel_id=1, source_target_pairs={{0,16},{1,17},{2,18},{3,19},{4,20},{5,21},{6,22},{7,23},{8,24},{9,... | collective-permute-start | bytes 2359304 | tf_op jit(solution)/shard_map/while/body/eval_jaxpr/ppermute | solution.py:18
  223.1 15.0 %collective-permute-start.1 = (bf16[128,1536]{1,0:T(8,128)(2,1)S(1)}, bf16[128,1536]{1,0:T(8,128)(2,1)S(1)}, u32[]{:S(2)}, u32[]{:S(2)}) collective-permute-start(bf16[128,1536]{1,0:T(8,128)(2,1)S(1)} %get-tuple-element.445), channel_id=1, source_target_pairs={{1,0},{2,1},{3,2},{4,3},{5,4},{6,5},{7,6},{8,7},{9,8},{10,9},{11,1... | collective-permute-start | bytes 1179656 | tf_op jit(solution)/shard_map/while/body/eval_jaxpr/ppermute | solution.py:18
  228.6 10.5 %collective-permute-start = (bf16[128,1536]{1,0:T(8,128)(2,1)S(1)}, bf16[128,1536]{1,0:T(8,128)(2,1)}, u32[]{:S(2)}, u32[]{:S(2)}) collective-permute-start(bf16[128,1536]{1,0:T(8,128)(2,1)S(1)} %get-tuple-element.445), channel_id=1, source_target_pairs={{0,1},{1,2},{2,3},{3,4},{4,5},{5,6},{6,7},{7,8},{8,9},{9,10},{10,1... | collective-permute-start | bytes 1179656 | tf_op jit(solution)/shard_map/while/body/eval_jaxpr/ppermute | solution.py:18
  248.0 3.3 %copy-start = (f32[6,64,12]{1,2,0:T(8,128)S(1)}, f32[6,64,12]{1,2,0:T(8,128)}, u32[]{:S(2)}) copy-start(f32[6,64,12]{1,2,0:T(8,128)} %add_rsqrt_fusion.1) | copy-start | bytes 55300 | tf_op jit(solution)/shard_map/while/body/eval_jaxpr/cond
  252.9 1.4 copy-start.2
  252.9 1.4 copy-start.3
  252.9 1.4 copy-start.4
  254.0 3.6 %slice-start = ((s8[9437184]{0:T(1024)(128)(4,1)}), s8[4194304]{0:T(1024)(128)(4,1)S(1)}, s32[]{:S(2)}) async-start(s8[9437184]{0:T(1024)(128)(4,1)} %bitcast.64), calls=%async_computation.1 | async-start | bytes 8388608 | tf_op jit(solution)/shard_map/while/body/eval_jaxpr/cond
  254.3 3.4 %slice-start.1 = ((s8[9437184]{0:T(1024)(128)(4,1)}), s8[4194304]{0:T(1024)(128)(4,1)S(1)}, s32[]{:S(2)}) async-start(s8[9437184]{0:T(1024)(128)(4,1)} %bitcast.64), calls=%async_computation.2 | async-start | bytes 8388608 | tf_op jit(solution)/shard_map/while/body/eval_jaxpr/cond
  255.1 1.5 copy-start.1
  256.6 1.5 slice-start.2
  262.2 18.3 %collective-permute-start.2 = (bf16[128,3072]{1,0:T(8,128)(2,1)}, bf16[128,3072]{1,0:T(8,128)(2,1)S(1)}, u32[]{:S(2)}, u32[]{:S(2)}) collective-permute-start(bf16[128,3072]{1,0:T(8,128)(2,1)} %get-tuple-element.446), channel_id=1, source_target_pairs={{0,16},{1,17},{2,18},{3,19},{4,20},{5,21},{6,22},{7,23},{8,24},{9,... | collective-permute-start | bytes 2359304 | tf_op jit(solution)/shard_map/while/body/eval_jaxpr/ppermute | solution.py:18
Sparse Core Ops, SparseCore 0:
  9.6 80.7 all-gather.2
where the time goes:
time: 292 us; the launch traced here: 287 us
  waiting for transfers between devices  177 us (61%)
  matrix products  29.8 us (10%)
  starting transfers between devices  23.1 us (8%)
  local copies, waits for them, and re-layouts  22.3 us (8%)
  other arithmetic  20.6 us (7%)
  between operations  13.4 us (5%)
    ppermute x9, waiting for transfers between devices, from_behind(): return lax.ppermute(value, axis, pairs)  94.7 us
    all_gather x1, waiting for transfers between devices, on_device(): weight = lax.all_gather(proj[0], 'dp', axis=0, tiled=True)  81.9 us
    ppermute x9, starting transfers between devices, from_behind(): return lax.ppermute(value, axis, pairs)  23.1 us
    dot_general x2, matrix products, project(): jnp.dot(normed, weight, preferred_element_type=jnp.float32)  10.2 us
    dot_general x2, matrix products, finish(): lax.dot_general(mixed, weight, (((1,), (1,)), ((), ())), preferred_elemen...  8.16 us
    dot_general x2, matrix products, attend(): jnp.einsum('qhsw,wjhd->qhsjd', onehot, vals_win, preferred_element_type=j...  6.22 us
  transfers between devices with their start and end apart: 10, of which 10 were waited for; matrix products, arithmetic and copies ran while one was open for 4% of the time, Pallas kernels for 0%

commit v1 on v0

v1 whole, which is shorter than its diff:
```python
import functools
import math

import jax
import jax.numpy as jnp
from jax import lax
from jax.experimental import pallas as pl
from jax.experimental.pallas import tpu as pltpu
from jax.sharding import PartitionSpec as P

BLOCK = 64
MESH = pl.DeviceIdType.MESH
NEG = -1e30
epsilon = 1e-06
PARTS = 4
TILE = 512


def at(start, size, step):
    return pl.ds(pl.multiple_of(start, step), size)


def kernel(
    cfg, lat_ref, proj_ref, scale_ref, bias_ref, out_ref,
    weight, hidden, acc, win, mix,
    ring_send, ring_recv, pair_send, pair_recv, halo_send, halo_recv, next_send, next_recv,
):
    segs, dps, micro, toks, heads = cfg
    rows, feats = proj_ref.shape
    width = lat_ref.shape[1]
    hd = feats // heads
    part = feats // PARTS
    half = feats // 2
    tiles = width // TILE
    n = dps // 2
    seg = lax.axis_index("segment")
    dp = lax.axis_index("dp")
    chip, core = lax.div(dp, 2), lax.rem(dp, 2)
    partner = dp + 1 - 2 * core

    odd = lax.rem(chip, 2)
    pos = lax.div(chip, 2) * (1 - odd) + (n - 1 - lax.div(chip, 2)) * odd

    def pair_at(p):
        p = lax.rem(p + 2 * n, n)
        back = lax.div(p, n // 2)
        return 2 * p * (1 - back) + (2 * (n - 1 - p) + 1) * back

    up = pair_at(pos + 1) * 2 + core
    down = pair_at(pos - 1) * 2 + core

    barrier = pltpu.get_barrier_semaphore()

    def greet(s, d):
        pl.semaphore_signal(barrier, inc=1, device_id=(s, d), device_id_type=MESH)

    greet(seg, up)
    greet(seg, down)
    greet(seg, partner)
    far = dp + 2 * core - 1
    has_far = (far >= 0) & (far < dps)

    @pl.when(has_far)
    def _():
        greet(seg, far)

    @pl.when(seg > 0)
    def _():
        greet(seg - 1, dp)

    @pl.when(seg < segs - 1)
    def _():
        greet(seg + 1, dp)

    peers = 3 + has_far.astype(jnp.int32) + (seg > 0).astype(jnp.int32)
    pl.semaphore_wait(barrier, peers + (seg < segs - 1).astype(jnp.int32))

    def owner(step, q):
        return pair_at(pos - step) if q < PARTS // 2 else pair_at(pos + step)

    def block(step, q, c):
        return weight.at[at((owner(step, q) * 2 + c) * rows, rows, rows), pl.ds(q * part, part)]

    def ring_copy(step, q):
        ref = block(step, q, core)
        return pltpu.make_async_remote_copy(
            src_ref=ref, dst_ref=ref, send_sem=ring_send.at[step, q], recv_sem=ring_recv.at[step, q],
            device_id=(seg, up if q < PARTS // 2 else down), device_id_type=MESH,
        )

    def pair_copy(step, q):
        ref = block(step, q, core)
        return pltpu.make_async_remote_copy(
            src_ref=ref, dst_ref=ref, send_sem=pair_send.at[step, q], recv_sem=pair_recv.at[step, q],
            device_id=(seg, partner), device_id_type=MESH,
        )

    def ring_arrived(step, q):
        ref = block(step + 1, q, core)
        pltpu.make_async_remote_copy(
            src_ref=ref, dst_ref=ref, send_sem=ring_send.at[step, q], recv_sem=ring_recv.at[step, q],
            device_id=(seg, up if q < PARTS // 2 else down), device_id_type=MESH,
        ).wait_recv()

    def pair_arrived(step, q):
        ref = block(step, q, 1 - core)
        pltpu.make_async_remote_copy(
            src_ref=ref, dst_ref=ref, send_sem=pair_send.at[step, q], recv_sem=pair_recv.at[step, q],
            device_id=(seg, partner), device_id_type=MESH,
        ).wait_recv()

    weight[at(dp * rows, rows, rows), :] = proj_ref[...]
    for q in range(PARTS):
        ring_copy(0, q).start()
    for q in range(PARTS):
        pair_copy(0, q).start()

    @pl.when(seg == 0)
    def _():
        hidden[...] = lat_ref[...]
        acc[...] = jnp.zeros_like(acc)

    @pl.when(dp == 0)
    def _():
        for m in range(micro):
            win[m, 0:toks, :] = jnp.zeros((toks, feats), jnp.bfloat16)

    @pl.when(dp == dps - 1)
    def _():
        for m in range(micro):
            win[m, 2 * toks : 3 * toks, :] = jnp.zeros((toks, feats), jnp.bfloat16)

    deep = 2 * rows
    beside = deep % 128 == 0

    def absorb(step):
        for q in range(PARTS):
            pair_arrived(step, q)
        if beside:
            @pl.when(seg == 0)
            def _():
                for side in range(2):
                    cols = pl.ds(side * half, half)
                    there = at(owner(step, side * (PARTS // 2)) * deep, deep, deep)
                    acc[:, cols] += jnp.dot(
                        hidden[:, there], weight[there, cols], preferred_element_type=jnp.float32
                    )

    def gather_step(step, carry):
        for q in (0, PARTS // 2, 1, PARTS // 2 + 1):
            ring_arrived(step, q)

            @pl.when(step < n - 2)
            def _():
                ring_copy(step + 1, q).start()

            pair_copy(step + 1, q).start()
        absorb(step)
        return carry

    lax.fori_loop(0, n - 1, gather_step, 0)
    absorb(n - 1)

    def lines(m):
        return pl.ds(m * toks, toks)

    def project(m, arrives):
        acc[lines(m), :] = jnp.zeros((toks, feats), jnp.float32)

        def one(t, carry):
            if arrives:
                handed(m, t).wait_recv()
            cols = at(t * TILE, TILE, TILE)
            acc[lines(m), :] += jnp.dot(
                hidden[lines(m), cols], weight[cols, :], preferred_element_type=jnp.float32
            )
            return carry

        lax.fori_loop(0, tiles, one, 0)

    def handed(m, t):
        cols = at(t * TILE, TILE, TILE)
        return pltpu.make_async_remote_copy(
            src_ref=out_ref.at[lines(m), cols], dst_ref=hidden.at[lines(m), cols],
            send_sem=next_send.at[m, t], recv_sem=next_recv.at[m, t],
            device_id=(lax.rem(seg + 1, segs), dp), device_id_type=MESH,
        )

    def halo(m, way):
        there = pl.ds(0, toks) if way == 0 else pl.ds(2 * toks, toks)
        return pltpu.make_async_remote_copy(
            src_ref=win.at[m, pl.ds(toks, toks)], dst_ref=win.at[m, there],
            send_sem=halo_send.at[m, way], recv_sem=halo_recv.at[m, way],
            device_id=(seg, lax.rem(dp + (1 if way == 0 else dps - 1), dps)), device_id_type=MESH,
        )

    def share(m):
        h = hidden[lines(m), :].astype(jnp.float32)
        rate = lax.rsqrt(jnp.mean(h * h, axis=-1, keepdims=True) + epsilon)
        win[m, toks : 2 * toks, :] = (acc[lines(m), :] * rate).astype(jnp.bfloat16)

        @pl.when(dp < dps - 1)
        def _():
            halo(m, 0).start()

        @pl.when(dp > 0)
        def _():
            halo(m, 1).start()

    row_at = lax.broadcasted_iota(jnp.int32, (toks, 3 * toks), 0)
    col_at = lax.broadcasted_iota(jnp.int32, (toks, 3 * toks), 1)
    group = 3 if heads % 3 == 0 else 1

    def attend(m):
        def some(g, carry):
            for j in range(group):
                head = g * group + j
                cols = at(head * hd, hd, hd)
                vals = win[m, :, cols]
                vf = vals.astype(jnp.float32)
                keys = (
                    vf * lax.rsqrt(jnp.mean(vf * vf, axis=-1, keepdims=True) + epsilon)
                ).astype(jnp.bfloat16)
                score = lax.dot_general(
                    keys[toks : 2 * toks], keys, (((1,), (1,)), ((), ())),
                    preferred_element_type=jnp.float32,
                )
                extra = bias_ref[m, head]
                extra = jnp.concatenate(
                    [
                        jnp.broadcast_to(extra[b : b + 1], (BLOCK, 3 * toks))
                        for b in range(toks // BLOCK)
                    ],
                    axis=0,
                )
                score = score * scale_ref[head] + extra
                score = jnp.where(col_at == row_at + toks, NEG, score)
                top = jnp.max(score, axis=-1, keepdims=True)
                grown = jnp.exp(score - top)
                total = jnp.sum(grown, axis=-1, keepdims=True)
                mixed = jnp.dot(
                    grown.astype(jnp.bfloat16), vals, preferred_element_type=jnp.float32
                )
                mix[:, cols] = (mixed / total).astype(jnp.bfloat16)
            return carry

        lax.fori_loop(0, heads // group, some, 0)

    def finish(m):
        def one(t, carry):
            cols = at(t * TILE, TILE, TILE)
            back = lax.dot_general(
                mix[...], weight[cols, :], (((1,), (1,)), ((), ())),
                preferred_element_type=jnp.float32,
            )
            out_ref[lines(m), cols] = (
                hidden[lines(m), cols].astype(jnp.float32) + back
            ).astype(jnp.bfloat16)

            @pl.when(seg < segs - 1)
            def _():
                handed(m, t).start()

            return carry

        lax.fori_loop(0, tiles, one, 0)

    @pl.when(seg == 0)
    def _():
        for m in range(micro):
            if not beside:
                project(m, False)
            share(m)

    for m in range(micro):
        @pl.when(seg > 0)
        def _():
            project(m, True)
            share(m)

        @pl.when(dp > 0)
        def _():
            halo(m, 0).wait_recv()

        @pl.when(dp < dps - 1)
        def _():
            halo(m, 1).wait_recv()

        attend(m)
        finish(m)

    def settle(step, carry):
        for q in range(PARTS):
            @pl.when(step < n - 1)
            def _():
                ring_copy(step, q).wait_send()

            pair_copy(step, q).wait_send()
        return carry

    lax.fori_loop(0, n, settle, 0)
    for m in range(micro):
        @pl.when(dp < dps - 1)
        def _():
            halo(m, 0).wait_send()

        @pl.when(dp > 0)
        def _():
            halo(m, 1).wait_send()

        @pl.when(seg < segs - 1)
        def _():
            for t in range(tiles):
                handed(m, t).wait_send()


def on_device(latents, proj, temper, blocks):
    segs = lax.axis_size("segment")
    dps = lax.axis_size("dp")
    dp = lax.axis_index("dp")
    micro, toks, width = latents.shape
    heads = temper.shape[1]
    rows, feats = proj.shape[1:]
    per_dev = toks // BLOCK
    total_blocks = toks * dps // BLOCK
    seq_blocks = min(4096, toks * dps) // BLOCK
    scale = temper[0] * (1.0 / math.sqrt(feats // heads))

    query = dp * per_dev + jnp.arange(per_dev, dtype=jnp.int32)
    absolute = (dp - 1) * per_dev + blocks
    usable = (
        (absolute >= 0)
        & (absolute < total_blocks)
        & (absolute // seq_blocks == (query // seq_blocks)[None, :, None, None])
    )
    spots = jnp.arange(3 * per_dev, dtype=jnp.int32)
    listed = (blocks[..., None] == spots) & usable[..., None]
    count = jnp.sum(listed.astype(jnp.float32), axis=3)
    own = (spots[None, :] == per_dev + jnp.arange(per_dev)[:, None]).astype(jnp.float32)
    count = count + own[None, :, None, :]
    bias = jnp.where(count > 0, jnp.log(jnp.maximum(count, 1.0)), NEG)
    bias = jnp.repeat(jnp.transpose(bias, (0, 2, 1, 3)), BLOCK, axis=-1)

    n = dps // 2
    tiles = width // TILE
    dma = pltpu.SemaphoreType.DMA
    vmem = pl.BlockSpec(memory_space=pltpu.VMEM)
    states = pl.pallas_call(
        functools.partial(kernel, (segs, dps, micro, toks, heads)),
        out_shape=jax.ShapeDtypeStruct((micro * toks, width), jnp.bfloat16),
        in_specs=[vmem, vmem, pl.BlockSpec(memory_space=pltpu.SMEM), vmem],
        out_specs=vmem,
        scratch_shapes=[
            pltpu.VMEM((rows * dps, feats), jnp.bfloat16),
            pltpu.VMEM((micro * toks, width), jnp.bfloat16),
            pltpu.VMEM((micro * toks, feats), jnp.float32),
            pltpu.VMEM((micro, 3 * toks, feats), jnp.bfloat16),
            pltpu.VMEM((toks, feats), jnp.bfloat16),
            dma((n - 1, PARTS)),
            dma((n - 1, PARTS)),
            dma((n, PARTS)),
            dma((n, PARTS)),
            dma((micro, 2)),
            dma((micro, 2)),
            dma((micro, tiles)),
            dma((micro, tiles)),
        ],
        compiler_params=pltpu.CompilerParams(
            collective_id=0, has_side_effects=True, vmem_limit_bytes=48 * 1024 * 1024
        ),
        cost_estimate=pl.CostEstimate(
            flops=4 * micro * toks * width * feats,
            bytes_accessed=2 * (rows * feats + 2 * micro * toks * width),
            transcendentals=micro * heads * toks * 3 * toks,
        ),
    )(latents.reshape(micro * toks, width), proj[0], scale, bias)
    return states.reshape(1, micro, toks, width)


def solution(mesh):
    placed = (
        P(None, "dp", None),
        P("segment", "dp", None),
        P("segment", None),
        P(None, "dp", None, None),
    )
    return jax.shard_map(
        on_device,
        mesh=mesh,
        in_specs=placed,
        out_specs=P("segment", None, "dp", None),
        check_vma=False,
    )
```

time: 292 us -> 129 us (0.44); the launches traced: 287 us -> 129 us
  waiting for transfers between devices: 177 us -> 0 us
  Pallas kernels: 0 us -> 122 us
  matrix products: 29.8 us -> 0 us
  starting transfers between devices: 23.1 us -> 0 us
  local copies, waits for them, and re-layouts: 22.3 us -> 3.95 us
  other arithmetic: 20.6 us -> 2.32 us
  between operations: 13.4 us -> 0.04 us
    pallas_call x0 -> x1, Pallas kernels: none -> 122 us  [on_device(): pl.pallas_call(functools.partial(kernel, (segs, dps, micro, toks, heads))...]
    ppermute x9 -> x0, waiting for transfers between devices: 94.7 us -> none  [from_behind(): return lax.ppermute(value, axis, pairs)]
    all_gather x1 -> x0, waiting for transfers between devices: 81.9 us -> none  [on_device(): weight = lax.all_gather(proj[0], 'dp', axis=0, tiled=True)]
    dot_general x12 -> x0, matrix products: 29.8 us -> none  [the longest x2 10.2 us: project(): jnp.dot(normed, weight, preferred_element_type=jnp.float32)]
    ppermute x9 -> x0, starting transfers between devices: 23.1 us -> none  [from_behind(): return lax.ppermute(value, axis, pairs)]
    cond x40 -> x0, local copies, waits for them, and re-layouts: 5.69 us -> none
    dynamic_update_slice x3 -> x0, other arithmetic: 5.5 us -> none  [one_turn(): lax.dynamic_update_index_in_dim(states, jnp.where(active, result, previou...]
    reshape x4 -> x1, local copies, waits for them, and re-layouts: 5.18 us -> 0.11 us  [on_device(): bias = jnp.repeat(jnp.transpose(bias, (0, 2, 1, 3)), BLOCK, axis=-1)]
  transfers between devices with their start and end apart: 10 -> 0, of which waited for: 10 -> 0; matrix products, arithmetic and copies ran while one was open for 4% -> 0% of each run, Pallas kernels for 0% -> 0%
where the time goes in v1:
time: 129 us
  Pallas kernels  122 us (95%)
  local copies, waits for them, and re-layouts  3.95 us (3%)
  other arithmetic  2.32 us (2%)
    pallas_call x1, Pallas kernels, on_device(): pl.pallas_call(functools.partial(kernel, (segs, dps, micro, toks, heads))...  122 us
    unnamed x5, local copies, waits for them, and re-layouts  3.61 us

profile of v1, /device:TPU:14, one launch (start us, length us, event | category | flops | bytes accessed | tf_op | source)
XLA Modules:
  0.0 128.6 jit_solution(4156403245947500400)
XLA Ops:
  0.0 0.7 multiply_bitcast_fusion.scale_ref
  0.7 0.1 compare_convert_fusion
  0.8 0.8 compare_and_fusion
  1.5 0.7 fusion
  2.2 0.1 select_bitcast_fusion
  2.3 0.1 copy.9
  2.4 0.1 broadcast_in_dim.6
  2.6 0.1 reshape.57.bias_ref
  2.7 0.0 copy-start
  2.7 1.4 %copy-done = bf16[2,128,3072]{2,1,0:T(8,128)(2,1)S(1)} copy-done((bf16[2,128,3072]{2,1,0:T(8,128)(2,1)S(1)}, bf16[2,128,3072]{2,1,0:T(8,128)(2,1)}, u32[]{:S(2)}) %copy-start) | copy-done | bytes 1572888
  4.1 0.0 copy-start.1
  4.1 1.1 copy-done.1
  5.2 122.3 %shard_map.46 = bf16[256,3072]{1,0:T(8,128)(2,1)S(1)} custom-call(bf16[256,3072]{1,0:T(8,128)(2,1)S(1)} %bitcast.8, bf16[192,1536]{1,0:T(8,128)(2,1)S(1)} %bitcast.9, f32[12]{0:T(128)S(1)} %multiply_bitcast_fusion.scale_ref, f32[2,12,2,384]{3,2,1,0:T(2,128)S(1)} %reshape.57.bias_ref), custom_call_target="tpu_custom_call" | custom-call | flops 4831838208 | bytes 3735552 | tf_op jit(solution)/shard_map/pallas_call | solution.py:348
  127.4 1.1 copy.11
  (2 shorter events, 0.0 us)
Async XLA Ops:
  2.7 1.4 %copy-start = (bf16[2,128,3072]{2,1,0:T(8,128)(2,1)S(1)}, bf16[2,128,3072]{2,1,0:T(8,128)(2,1)}, u32[]{:S(2)}) copy-start(bf16[2,128,3072]{2,1,0:T(8,128)(2,1)} %param.4) | copy-start | bytes 4718596
  4.1 1.1 copy-start.1

commit v2 on v1

--- a/solution.py
+++ b/solution.py
@@ -21,13 +21,13 @@
 
 
 def kernel(
-    cfg, lat_ref, proj_ref, scale_ref, bias_ref, out_ref,
-    weight, hidden, acc, win, mix,
+    cfg, temper_ref, blocks_ref, lat_ref, proj_ref, out_ref,
+    weight, hidden, acc, win, own_keys, mix, load_sem,
     ring_send, ring_recv, pair_send, pair_recv, halo_send, halo_recv, next_send, next_recv,
 ):
     segs, dps, micro, toks, heads = cfg
-    rows, feats = proj_ref.shape
-    width = lat_ref.shape[1]
+    rows, feats = proj_ref.shape[1:]
+    width = lat_ref.shape[2]
     hd = feats // heads
     part = feats // PARTS
     half = feats // 2
@@ -49,6 +49,21 @@
     up = pair_at(pos + 1) * 2 + core
     down = pair_at(pos - 1) * 2 + core
 
+    own_rows = pltpu.make_async_copy(
+        proj_ref.at[0], weight.at[at(dp * rows, rows, rows), :], load_sem.at[0]
+    )
+    own_rows.start()
+
+    def latent(m):
+        return pltpu.make_async_copy(
+            lat_ref.at[m], hidden.at[pl.ds(m * toks, toks)], load_sem.at[1 + m]
+        )
+
+    @pl.when(seg == 0)
+    def _():
+        for m in range(micro):
+            latent(m).start()
+
     barrier = pltpu.get_barrier_semaphore()
 
     def greet(s, d):
@@ -74,6 +89,8 @@
 
     peers = 3 + has_far.astype(jnp.int32) + (seg > 0).astype(jnp.int32)
     pl.semaphore_wait(barrier, peers + (seg < segs - 1).astype(jnp.int32))
+
+    own_rows.wait()
 
     def owner(step, q):
         return pair_at(pos - step) if q < PARTS // 2 else pair_at(pos + step)
@@ -109,7 +126,6 @@
             device_id=(seg, partner), device_id_type=MESH,
         ).wait_recv()
 
-    weight[at(dp * rows, rows, rows), :] = proj_ref[...]
     for q in range(PARTS):
         ring_copy(0, q).start()
     for q in range(PARTS):
@@ -117,7 +133,8 @@
 
     @pl.when(seg == 0)
     def _():
-        hidden[...] = lat_ref[...]
+        for m in range(micro):
+            latent(m).wait()
         acc[...] = jnp.zeros_like(acc)
 
     @pl.when(dp == 0)
@@ -186,71 +203,111 @@
             device_id=(lax.rem(seg + 1, segs), dp), device_id_type=MESH,
         )
 
-    def halo(m, way):
+    def halo(m, way, piece):
         there = pl.ds(0, toks) if way == 0 else pl.ds(2 * toks, toks)
+        cols = pl.ds(piece * half, half)
         return pltpu.make_async_remote_copy(
-            src_ref=win.at[m, pl.ds(toks, toks)], dst_ref=win.at[m, there],
-            send_sem=halo_send.at[m, way], recv_sem=halo_recv.at[m, way],
+            src_ref=win.at[m, pl.ds(toks, toks), cols], dst_ref=win.at[m, there, cols],
+            send_sem=halo_send.at[m, way, piece], recv_sem=halo_recv.at[m, way, piece],
             device_id=(seg, lax.rem(dp + (1 if way == 0 else dps - 1), dps)), device_id_type=MESH,
         )
+
+    ones = jnp.ones((hd, hd), jnp.bfloat16)
+
+    def unit(vals):
+        vf = vals.astype(jnp.float32)
+        squares = jnp.dot((vf * vf).astype(jnp.bfloat16), ones, preferred_element_type=jnp.float32)
+        return (vf * lax.rsqrt(squares * (1.0 / hd) + epsilon)).astype(jnp.bfloat16)
 
     def share(m):
         h = hidden[lines(m), :].astype(jnp.float32)
         rate = lax.rsqrt(jnp.mean(h * h, axis=-1, keepdims=True) + epsilon)
-        win[m, toks : 2 * toks, :] = (acc[lines(m), :] * rate).astype(jnp.bfloat16)
-
-        @pl.when(dp < dps - 1)
-        def _():
-            halo(m, 0).start()
-
-        @pl.when(dp > 0)
-        def _():
-            halo(m, 1).start()
-
-    row_at = lax.broadcasted_iota(jnp.int32, (toks, 3 * toks), 0)
-    col_at = lax.broadcasted_iota(jnp.int32, (toks, 3 * toks), 1)
-    group = 3 if heads % 3 == 0 else 1
+        for piece in range(2):
+            cols = pl.ds(piece * half, half)
+            win[m, toks : 2 * toks, cols] = (acc[lines(m), cols] * rate).astype(jnp.bfloat16)
+
+            @pl.when(dp < dps - 1)
+            def _():
+                halo(m, 0, piece).start()
+
+            @pl.when(dp > 0)
+            def _():
+                halo(m, 1, piece).start()
+
+    def prepare(m):
+        def one(head, carry):
+            cols = at(head * hd, hd, hd)
+            own_keys[m, :, cols] = unit(win[m, toks : 2 * toks, cols])
+            return carry
+
+        lax.fori_loop(0, heads, one, 0)
+
+    per_dev = toks // BLOCK
+    seq_blocks = min(4096, toks * dps) // BLOCK
+    diagonal = lax.broadcasted_iota(jnp.int32, (toks, toks), 0) == lax.broadcasted_iota(
+        jnp.int32, (toks, toks), 1
+    )
+    spot = lax.div(lax.broadcasted_iota(jnp.int32, (1, 3 * toks), 1), BLOCK)
+    home = lax.div(dp * per_dev, seq_blocks)
+    first = home * seq_blocks - (dp - 1) * per_dev
+    last = jnp.minimum((home + 1) * seq_blocks, dps * per_dev) - (dp - 1) * per_dev
+    inside = (spot >= first) & (spot < last)
+    group = 3 if heads % 6 == 0 else 1
+    log2e = 1.4426950408889634
+
+    def listed(m, head, b):
+        count = jnp.zeros((1, 3 * toks), jnp.int32)
+        for s in range(blocks_ref.shape[3]):
+            count += (spot == blocks_ref[m, b, head, s]).astype(jnp.int32)
+        count = jnp.where(inside, count, 0) + (spot == per_dev + b).astype(jnp.int32)
+        return jnp.where(count > 0, jnp.log2(jnp.maximum(count, 1).astype(jnp.float32)), NEG)
 
     def attend(m):
-        def some(g, carry):
-            for j in range(group):
-                head = g * group + j
-                cols = at(head * hd, hd, hd)
-                vals = win[m, :, cols]
-                vf = vals.astype(jnp.float32)
-                keys = (
-                    vf * lax.rsqrt(jnp.mean(vf * vf, axis=-1, keepdims=True) + epsilon)
-                ).astype(jnp.bfloat16)
-                score = lax.dot_general(
-                    keys[toks : 2 * toks], keys, (((1,), (1,)), ((), ())),
-                    preferred_element_type=jnp.float32,
-                )
-                extra = bias_ref[m, head]
-                extra = jnp.concatenate(
-                    [
-                        jnp.broadcast_to(extra[b : b + 1], (BLOCK, 3 * toks))
-                        for b in range(toks // BLOCK)
-                    ],
-                    axis=0,
-                )
-                score = score * scale_ref[head] + extra
-                score = jnp.where(col_at == row_at + toks, NEG, score)
-                top = jnp.max(score, axis=-1, keepdims=True)
-                grown = jnp.exp(score - top)
-                total = jnp.sum(grown, axis=-1, keepdims=True)
-                mixed = jnp.dot(
-                    grown.astype(jnp.bfloat16), vals, preferred_element_type=jnp.float32
-                )
-                mix[:, cols] = (mixed / total).astype(jnp.bfloat16)
-            return carry
-
-        lax.fori_loop(0, heads // group, some, 0)
+        def one_head(head):
+            cols = at(head * hd, hd, hd)
+            vals = win[m, :, cols]
+            query = own_keys[m, :, cols]
+            keys = jnp.concatenate([unit(vals[:toks]), query, unit(vals[2 * toks :])], axis=0)
+            score = lax.dot_general(
+                query, keys, (((1,), (1,)), ((), ())), preferred_element_type=jnp.float32
+            )
+            scale = temper_ref[0, head] * (log2e / math.sqrt(hd))
+            score = jnp.concatenate(
+                [
+                    score[b * BLOCK : (b + 1) * BLOCK] * scale + listed(m, head, b)
+                    for b in range(per_dev)
+                ],
+                axis=0,
+            )
+            own = jnp.where(diagonal, NEG, score[:, toks : 2 * toks])
+            score = jnp.concatenate([score[:, :toks], own, score[:, 2 * toks :]], axis=1)
+            top = jnp.max(score, axis=-1, keepdims=True)
+            grown = jnp.exp2(score - top).astype(jnp.bfloat16)
+            wide = jnp.concatenate([vals, jnp.ones((3 * toks, hd), jnp.bfloat16)], axis=1)
+            both = jnp.dot(grown, wide, preferred_element_type=jnp.float32)
+            mix[m, :, cols] = (both[:, :hd] / both[:, hd:]).astype(jnp.bfloat16)
+
+        for piece in range(2):
+            @pl.when(dp > 0)
+            def _():
+                halo(m, 0, piece).wait_recv()
+
+            @pl.when(dp < dps - 1)
+            def _():
+                halo(m, 1, piece).wait_recv()
+
+            def some(g, carry):
+                for j in range(group):
+                    one_head(piece * (heads // 2) + g * group + j)
+                return carry
+
+            lax.fori_loop(0, heads // 2 // group, some, 0)
 
     def finish(m):
         def one(t, carry):
             cols = at(t * TILE, TILE, TILE)
             back = lax.dot_general(
-                mix[...], weight[cols, :], (((1,), (1,)), ((), ())),
+                mix[m], weight[cols, :], (((1,), (1,)), ((), ())),
                 preferred_element_type=jnp.float32,
             )
             out_ref[lines(m), cols] = (
@@ -271,23 +328,21 @@
             if not beside:
                 project(m, False)
             share(m)
-
-    for m in range(micro):
-        @pl.when(seg > 0)
-        def _():
+        for m in range(micro):
+            prepare(m)
+            attend(m)
+            finish(m)
+
+    @pl.when(seg > 0)
+    def _():
+        for m in range(micro):
             project(m, True)
             share(m)
-
-        @pl.when(dp > 0)
-        def _():
-            halo(m, 0).wait_recv()
-
-        @pl.when(dp < dps - 1)
-        def _():
-            halo(m, 1).wait_recv()
-
-        attend(m)
-        finish(m)
+            prepare(m)
+            if m > 0:
+                finish(m - 1)
+            attend(m)
+        finish(micro - 1)
 
     def settle(step, carry):
         for q in range(PARTS):
@@ -302,11 +357,13 @@
     for m in range(micro):
         @pl.when(dp < dps - 1)
         def _():
-            halo(m, 0).wait_send()
+            for piece in range(2):
+                halo(m, 0, piece).wait_send()
 
         @pl.when(dp > 0)
         def _():
-            halo(m, 1).wait_send()
+            for piece in range(2):
+                halo(m, 1, piece).wait_send()
 
         @pl.when(seg < segs - 1)
         def _():
@@ -317,63 +374,46 @@
 def on_device(latents, proj, temper, blocks):
     segs = lax.axis_size("segment")
     dps = lax.axis_size("dp")
-    dp = lax.axis_index("dp")
     micro, toks, width = latents.shape
     heads = temper.shape[1]
     rows, feats = proj.shape[1:]
-    per_dev = toks // BLOCK
-    total_blocks = toks * dps // BLOCK
-    seq_blocks = min(4096, toks * dps) // BLOCK
-    scale = temper[0] * (1.0 / math.sqrt(feats // heads))
-
-    query = dp * per_dev + jnp.arange(per_dev, dtype=jnp.int32)
-    absolute = (dp - 1) * per_dev + blocks
-    usable = (
-        (absolute >= 0)
-        & (absolute < total_blocks)
-        & (absolute // seq_blocks == (query // seq_blocks)[None, :, None, None])
-    )
-    spots = jnp.arange(3 * per_dev, dtype=jnp.int32)
-    listed = (blocks[..., None] == spots) & usable[..., None]
-    count = jnp.sum(listed.astype(jnp.float32), axis=3)
-    own = (spots[None, :] == per_dev + jnp.arange(per_dev)[:, None]).astype(jnp.float32)
-    count = count + own[None, :, None, :]
-    bias = jnp.where(count > 0, jnp.log(jnp.maximum(count, 1.0)), NEG)
-    bias = jnp.repeat(jnp.transpose(bias, (0, 2, 1, 3)), BLOCK, axis=-1)
-
     n = dps // 2
     tiles = width // TILE
     dma = pltpu.SemaphoreType.DMA
     vmem = pl.BlockSpec(memory_space=pltpu.VMEM)
+    smem = pl.BlockSpec(memory_space=pltpu.SMEM)
+    anywhere = pl.BlockSpec(memory_space=pl.ANY)
     states = pl.pallas_call(
         functools.partial(kernel, (segs, dps, micro, toks, heads)),
         out_shape=jax.ShapeDtypeStruct((micro * toks, width), jnp.bfloat16),
-        in_specs=[vmem, vmem, pl.BlockSpec(memory_space=pltpu.SMEM), vmem],
+        in_specs=[smem, smem, anywhere, anywhere],
         out_specs=vmem,
         scratch_shapes=[
             pltpu.VMEM((rows * dps, feats), jnp.bfloat16),
             pltpu.VMEM((micro * toks, width), jnp.bfloat16),
             pltpu.VMEM((micro * toks, feats), jnp.float32),
             pltpu.VMEM((micro, 3 * toks, feats), jnp.bfloat16),
-            pltpu.VMEM((toks, feats), jnp.bfloat16),
+            pltpu.VMEM((micro, toks, feats), jnp.bfloat16),
+            pltpu.VMEM((micro, toks, feats), jnp.bfloat16),
+            dma((1 + micro,)),
             dma((n - 1, PARTS)),
             dma((n - 1, PARTS)),
             dma((n, PARTS)),
             dma((n, PARTS)),
-            dma((micro, 2)),
-            dma((micro, 2)),
+            dma((micro, 2, 2)),
+            dma((micro, 2, 2)),
             dma((micro, tiles)),
             dma((micro, tiles)),
         ],
         compiler_params=pltpu.CompilerParams(
-            collective_id=0, has_side_effects=True, vmem_limit_bytes=48 * 1024 * 1024
+            collective_id=0, has_side_effects=True, vmem_limit_bytes=62 * 1024 * 1024
         ),
         cost_estimate=pl.CostEstimate(
             flops=4 * micro * toks * width * feats,
             bytes_accessed=2 * (rows * feats + 2 * micro * toks * width),
             transcendentals=micro * heads * toks * 3 * toks,
         ),
-    )(latents.reshape(micro * toks, width), proj[0], scale, bias)
+    )(temper, blocks, latents, proj)
     return states.reshape(1, micro, toks, width)
 
 

time: 129 us -> 121 us (0.938)
  Pallas kernels: 122 us -> 117 us
  other arithmetic: 2.32 us -> 0 us
    pallas_call x1, Pallas kernels: 122 us -> 117 us  [on_device(): pl.pallas_call(functools.partial(kernel, (segs, dps, micro, toks, heads))...]
    unnamed x5 -> x2, local copies, waits for them, and re-layouts: 3.61 us -> 4.05 us
where the time goes in v2:
time: 121 us
  Pallas kernels  117 us (97%)
  local copies, waits for them, and re-layouts  4.05 us (3%)
    pallas_call x1, Pallas kernels, on_device(): pl.pallas_call(functools.partial(kernel, (segs, dps, micro, toks, heads))...  117 us
    unnamed x2, local copies, waits for them, and re-layouts  4.05 us

profile of v2, /device:TPU:14, one launch (start us, length us, event | category | flops | bytes accessed | tf_op | source)
XLA Modules:
  0.0 120.6 jit_solution(14808232064905916951)
XLA Ops:
  0.0 1.4 %copy.5.blocks_ref = s32[2,2,12,2]{3,2,1,0:T(8,128)} copy(s32[2,2,12,2]{2,3,1,0:T(2,128)} %param.7) | data formatting | bytes 768 | tf_op args[3]
  1.4 116.6 %shard_map.46 = bf16[256,3072]{1,0:T(8,128)(2,1)} custom-call(f32[1,12]{1,0:T(1,128)} %temper_ref.1, s32[2,2,12,2]{3,2,1,0:T(8,128)} %copy.5.blocks_ref, bf16[2,128,3072]{2,1,0:T(8,128)(2,1)} %lat_ref.1, bf16[1,192,1536]{2,1,0:T(8,128)(2,1)} %proj_ref.1), custom_call_target="tpu_custom_call" | custom-call | flops 4831838208 | bytes 3735552 | tf_op jit(solution)/shard_map/pallas_call | solution.py:386
  118.0 2.7 %copy.7 = bf16[1,2,128,3072]{3,2,1,0:T(8,128)(2,1)} copy(bf16[1,2,128,3072]{3,2,1,0:T(8,128)(2,1)} %bitcast.1) | data formatting | bytes 3145728

commit v3 on v2

--- a/solution.py
+++ b/solution.py
@@ -181,10 +181,14 @@
     def lines(m):
         return pl.ds(m * toks, toks)
 
+    lead = 4 * tiles // 6
+
     def project(m, arrives):
         acc[lines(m), :] = jnp.zeros((toks, feats), jnp.float32)
 
-        def one(t, carry):
+        def one(finishing, t, carry):
+            if finishing:
+                finish_piece(m - 1, t)
             if arrives:
                 handed(m, t).wait_recv()
             cols = at(t * TILE, TILE, TILE)
@@ -193,7 +197,11 @@
             )
             return carry
 
-        lax.fori_loop(0, tiles, one, 0)
+        if arrives and m > 0:
+            lax.fori_loop(0, lead, functools.partial(one, True), 0)
+            lax.fori_loop(lead, tiles, functools.partial(one, False), 0)
+        else:
+            lax.fori_loop(0, tiles, functools.partial(one, False), 0)
 
     def handed(m, t):
         cols = at(t * TILE, TILE, TILE)
@@ -303,24 +311,26 @@
 
             lax.fori_loop(0, heads // 2 // group, some, 0)
 
-    def finish(m):
+    def finish_piece(m, t):
+        cols = at(t * TILE, TILE, TILE)
+        back = lax.dot_general(
+            mix[m], weight[cols, :], (((1,), (1,)), ((), ())),
+            preferred_element_type=jnp.float32,
+        )
+        out_ref[lines(m), cols] = (
+            hidden[lines(m), cols].astype(jnp.float32) + back
+        ).astype(jnp.bfloat16)
+
+        @pl.when(seg < segs - 1)
+        def _():
+            handed(m, t).start()
+
+    def finish(m, begin=0):
         def one(t, carry):
-            cols = at(t * TILE, TILE, TILE)
-            back = lax.dot_general(
-                mix[m], weight[cols, :], (((1,), (1,)), ((), ())),
-                preferred_element_type=jnp.float32,
-            )
-            out_ref[lines(m), cols] = (
-                hidden[lines(m), cols].astype(jnp.float32) + back
-            ).astype(jnp.bfloat16)
-
-            @pl.when(seg < segs - 1)
-            def _():
-                handed(m, t).start()
-
+            finish_piece(m, t)
             return carry
 
-        lax.fori_loop(0, tiles, one, 0)
+        lax.fori_loop(begin, tiles, one, 0)
 
     @pl.when(seg == 0)
     def _():
@@ -340,7 +350,7 @@
             share(m)
             prepare(m)
             if m > 0:
-                finish(m - 1)
+                finish(m - 1, lead)
             attend(m)
         finish(micro - 1)
 

time: 121 us -> 123 us (1.017)
  Pallas kernels: 117 us -> 119 us
    pallas_call x1, Pallas kernels: 117 us -> 119 us  [on_device(): pl.pallas_call(functools.partial(kernel, (segs, dps, micro, toks, heads))...]
where the time goes in v3:
time: 123 us
  Pallas kernels  119 us (97%)
  local copies, waits for them, and re-layouts  4.05 us (3%)
    pallas_call x1, Pallas kernels, on_device(): pl.pallas_call(functools.partial(kernel, (segs, dps, micro, toks, heads))...  119 us
    unnamed x2, local copies, waits for them, and re-layouts  4.05 us

profile of v3, /device:TPU:14, one launch (start us, length us, event | category | flops | bytes accessed | tf_op | source)
XLA Modules:
  0.0 123.2 jit_solution(12581594665295295023)
XLA Ops:
  0.0 1.4 %copy.5.blocks_ref = s32[2,2,12,2]{3,2,1,0:T(8,128)} copy(s32[2,2,12,2]{2,3,1,0:T(2,128)} %param.7) | data formatting | bytes 768 | tf_op args[3]
  1.4 119.2 %shard_map.46 = bf16[256,3072]{1,0:T(8,128)(2,1)} custom-call(f32[1,12]{1,0:T(1,128)} %temper_ref.1, s32[2,2,12,2]{3,2,1,0:T(8,128)} %copy.5.blocks_ref, bf16[2,128,3072]{2,1,0:T(8,128)(2,1)} %lat_ref.1, bf16[1,192,1536]{2,1,0:T(8,128)(2,1)} %proj_ref.1), custom_call_target="tpu_custom_call" | custom-call | flops 4831838208 | bytes 3735552 | tf_op jit(solution)/shard_map/pallas_call | solution.py:396
  120.6 2.7 %copy.7 = bf16[1,2,128,3072]{3,2,1,0:T(8,128)(2,1)} copy(bf16[1,2,128,3072]{3,2,1,0:T(8,128)(2,1)} %bitcast.1) | data formatting | bytes 3145728

commit v4 on v2

--- a/solution.py
+++ b/solution.py
@@ -303,7 +303,7 @@
 
             lax.fori_loop(0, heads // 2 // group, some, 0)
 
-    def finish(m):
+    def finish(m, begin=0, end=tiles):
         def one(t, carry):
             cols = at(t * TILE, TILE, TILE)
             back = lax.dot_general(
@@ -320,7 +320,26 @@
 
             return carry
 
-        lax.fori_loop(0, tiles, one, 0)
+        lax.fori_loop(begin, end, one, 0)
+
+    lead = 2
+
+    def finish_two(begin):
+        both = pl.ds((micro - 2) * toks, 2 * toks)
+        mixed = mix[micro - 2 : micro].reshape(2 * toks, feats)
+
+        def one(t, carry):
+            cols = at(t * TILE, TILE, TILE)
+            back = lax.dot_general(
+                mixed, weight[cols, :], (((1,), (1,)), ((), ())),
+                preferred_element_type=jnp.float32,
+            )
+            out_ref[both, cols] = (hidden[both, cols].astype(jnp.float32) + back).astype(
+                jnp.bfloat16
+            )
+            return carry
+
+        lax.fori_loop(begin, tiles, one, 0)
 
     @pl.when(seg == 0)
     def _():
@@ -339,10 +358,27 @@
             project(m, True)
             share(m)
             prepare(m)
-            if m > 0:
+            if 0 < m < micro - 1:
                 finish(m - 1)
+            elif m > 0:
+                finish(m - 1, 0, lead)
+
+                @pl.when(seg < segs - 1)
+                def _():
+                    finish(m - 1, lead)
+
             attend(m)
-        finish(micro - 1)
+        if micro > 1:
+            @pl.when(seg < segs - 1)
+            def _():
+                finish(micro - 1)
+
+            @pl.when(seg == segs - 1)
+            def _():
+                finish_two(lead)
+                finish(micro - 1, 0, lead)
+        else:
+            finish(0)
 
     def settle(step, carry):
         for q in range(PARTS):

time: 121 us -> 121 us (level)
  no operation moved by 1% of the time
where the time goes in v4:
time: 121 us; the launch traced here: 120 us
  Pallas kernels  116 us (96%)
  local copies, waits for them, and re-layouts  4.05 us (3%)
    pallas_call x1, Pallas kernels, on_device(): pl.pallas_call(functools.partial(kernel, (segs, dps, micro, toks, heads))...  116 us
    unnamed x2, local copies, waits for them, and re-layouts  4.05 us

profile of v4, /device:TPU:14, one launch (start us, length us, event | category | flops | bytes accessed | tf_op | source)
XLA Modules:
  0.0 120.5 jit_solution(9863248477844706356)
XLA Ops:
  0.0 1.4 %copy.5.blocks_ref = s32[2,2,12,2]{3,2,1,0:T(8,128)} copy(s32[2,2,12,2]{2,3,1,0:T(2,128)} %param.7) | data formatting | bytes 768 | tf_op args[3]
  1.4 116.4 %shard_map.46 = bf16[256,3072]{1,0:T(8,128)(2,1)} custom-call(f32[1,12]{1,0:T(1,128)} %temper_ref.1, s32[2,2,12,2]{3,2,1,0:T(8,128)} %copy.5.blocks_ref, bf16[2,128,3072]{2,1,0:T(8,128)(2,1)} %lat_ref.1, bf16[1,192,1536]{2,1,0:T(8,128)(2,1)} %proj_ref.1), custom_call_target="tpu_custom_call" | custom-call | flops 4831838208 | bytes 3735552 | tf_op jit(solution)/shard_map/pallas_call | solution.py:422
  117.8 2.7 %copy.7 = bf16[1,2,128,3072]{3,2,1,0:T(8,128)(2,1)} copy(bf16[1,2,128,3072]{3,2,1,0:T(8,128)(2,1)} %bitcast.1) | data formatting | bytes 3145728
